TPU v7x, 1024 devices: a whole 4x8x16 slice. The times are simulated.
1024 devices in a mesh: dp: 8 (over y), ctx: 16 (over z_hi, x, core), tp: 8 (over z_lo).
Axes of the slice: x: 4, y: 8, z: 16 (z_hi: 2, z_lo: 8; z = z_hi * 8 + z_lo), core: 2. Of those that a mesh axis runs over, the one named last changes fastest.
Arguments:
- tokens: bfloat16 [16384, 6144], P(('dp', 'ctx')), may hold values from -6 to 6
- router_weight: bfloat16 [6144, 16], replicated, may hold values from -0.15625 to 0.15625
- expert_hidden: bfloat16 [8, 56, 16, 16, 5376], P('dp', None, 'ctx', None, 'tp'), may hold values from -6 to 6
- down_weight: bfloat16 [16, 5376, 3072], P('ctx', 'tp'), may hold values from -0.109375 to 0.109375
- expert_ids: int32 [16384, 4], P(('dp', 'ctx')), may hold values from 0 to 15, as said below
- mixed_grad: bfloat16 [16384, 3072], P(('dp', 'ctx')), may hold values from -6 to 6
Outputs:
- combined: bfloat16 [16384, 3072], P(('dp', 'ctx'), 'tp')
- row_grads: bfloat16 [8, 56, 16, 16, 3072], P('dp', None, 'ctx', None, 'tp')
- router_grad: float32 [6144, 16], replicated
Inputs may be any that keep to these rules, and one draw needn't show every extreme that they name: `expert_ids`: each token names 4 different experts. Among the 128 tokens of one index of dp and ctx no expert is named by more than 56 tokens, and one expert, the same for all such groups, is named by exactly 56 of them in every group.
All inputs are finite; a program needn't handle non-finite values.
Results may differ from a plain program's by a relative error of at most 0.02.
Values may be sent and summed in bfloat16 or wider, within the bound.
A program may use at most 64 MiB of HBM per device.

v0:
```python
import jax
import jax.numpy as jnp
from jax import lax
from jax.sharding import PartitionSpec as P


def round_term(values):
    rounded = lax.optimization_barrier(values.astype(jnp.bfloat16))
    return rounded.astype(jnp.float32)


def spread_grad(gate_values, gate_grad, onehot):
    mix_term = jnp.sum(gate_values * gate_grad, axis=1, keepdims=True)
    chosen_grad = gate_values * (gate_grad - mix_term)
    return jnp.sum(jnp.where(onehot, chosen_grad[:, :, None], 0.0), axis=1)


def per_device(tokens, router_weight, expert_hidden, down_weight, expert_ids, mixed_grad):
    tp_ranks = lax.axis_size("tp")
    tp_index = lax.axis_index("tp")
    hidden = expert_hidden[0]
    capacity = hidden.shape[0]
    experts_all = router_weight.shape[1]
    full_width = mixed_grad.shape[1]
    col_width = full_width // tp_ranks
    tok_count = tokens.shape[0]
    top_count = expert_ids.shape[1]
    logits = jnp.dot(tokens, router_weight, preferred_element_type=jnp.float32)
    onehot = expert_ids[:, :, None] == jnp.arange(experts_all, dtype=jnp.int32)[None, None, :]
    chosen = jnp.sum(jnp.where(onehot, logits[:, None, :], 0.0), axis=2)
    weights = jnp.exp(chosen)
    gate_values = weights / jnp.sum(weights, axis=1, keepdims=True)
    flat_hits = onehot.reshape(tok_count * top_count, experts_all).astype(jnp.int32)
    before = jnp.cumsum(flat_hits, axis=0) - flat_hits
    slot_index = jnp.sum(before * flat_hits, axis=1).reshape(tok_count, top_count)
    route_index = (slot_index * experts_all + expert_ids).reshape(-1)
    grad_cols = lax.dynamic_slice_in_dim(mixed_grad, tp_index * col_width, col_width, 1)
    partial_sum = jnp.einsum(
        "cesf,efd->cesd", hidden, down_weight, preferred_element_type=jnp.float32
    )
    summed = lax.psum_scatter(
        round_term(partial_sum).astype(jnp.bfloat16), "tp", scatter_dimension=3, tiled=True
    )
    arrived = lax.all_to_all(summed, "ctx", split_axis=2, concat_axis=1, tiled=True)
    row_table = arrived.reshape(capacity * experts_all, col_width)
    picked = (
        jnp.take(row_table, route_index, axis=0)
        .reshape(tok_count, top_count, col_width)
        .astype(jnp.float32)
    )
    combined = jnp.einsum("tk,tkd->td", gate_values, picked).astype(jnp.bfloat16)
    gate_part = jnp.einsum("tkd,td->tk", picked, grad_cols.astype(jnp.float32))
    token_wide = tokens.astype(jnp.float32)
    logit_grad = spread_grad(gate_values, gate_part, onehot)
    partial_router = jnp.dot(token_wide.T, logit_grad, precision=lax.Precision.HIGHEST)
    router_total = lax.psum(partial_router, ("dp", "ctx", "tp"))
    router_grad = router_total / tok_count
    grad_values = (gate_values[:, :, None] * grad_cols[:, None, :].astype(jnp.float32)).astype(
        jnp.bfloat16
    )
    buffer = jnp.zeros((capacity * experts_all, col_width), jnp.bfloat16)
    buffer = buffer.at[route_index].set(grad_values.reshape(-1, col_width))
    outgoing = buffer.reshape(capacity, experts_all, 1, col_width)
    incoming = lax.all_to_all(outgoing, "ctx", split_axis=1, concat_axis=2, tiled=True)
    row_grads = incoming[None]
    return (combined, row_grads, router_grad)


def solution(mesh):
    return jax.shard_map(
        per_device,
        mesh=mesh,
        in_specs=(
            P(("dp", "ctx"), None),
            P(),
            P("dp", None, "ctx", None, "tp"),
            P("ctx", "tp", None),
            P(("dp", "ctx"), None),
            P(("dp", "ctx"), None),
        ),
        out_specs=(P(("dp", "ctx"), "tp"), P("dp", None, "ctx", None, "tp"), P()),
        check_vma=False,
    )
```

profile of v0, /device:TPU:6, one launch (start us, length us, event | category | flops | bytes accessed | tf_op | source)
XLA Modules:
  0.0 760.2 jit_solution(15753734422239472288)
XLA Ops:
  7.2 9.5 %convert_bitcast_fusion = bf16[56,1,16,3072]{3,0,2,1:T(8,128)(2,1)} fusion(bf16[1,672,3072]{2,1,0:T(8,128)(2,1)} %param.9, bf16[56,16,672]{2,1,0:T(8,128)(2,1)} %bitcast.68), kind=kOutput, calls=%fused_computation.3 | convolution fusion | flops 3702128640 | bytes 10838016 | tf_op jit(solution)/shard_map/cesf,efd->cesd/dot_general | solution.py:38
  16.7 15.3 %copy.68 = bf16[56,1,16,3072]{0,2,1,3:T(8,128)(2,1)} copy(bf16[56,1,16,3072]{3,0,2,1:T(8,128)(2,1)} %convert_bitcast_fusion) | data formatting | bytes 11010048
  32.0 19.2 %reshape.146 = bf16[3072,896]{1,0:T(8,128)(2,1)} reshape(bf16[3072,1,16,56]{3,2,1,0:T(8,128)(2,1)} %bitcast.58) | data formatting | bytes 11010048
  51.2 140.8 %reduce-scatter.4.cloned.1.call-done = bf16[384,896]{1,0:T(8,128)(2,1)} async-done(((bf16[3072,896]{1,0:T(8,128)(2,1)}), bf16[384,896]{1,0:T(8,128)(2,1)}) %reduce-scatter.4.cloned.1.call-update) | async-done | bytes 688144
  192.1 3.7 reshape.147
  195.8 1.8 copy.69
  197.6 8.5 %all-to-all-start = ((bf16[56,1,16,384]{3,0,1,2:T(8,128)(2,1)}), bf16[56,1,16,384]{3,0,1,2:T(8,128)(2,1)}, u32[]{:S(2)}, u32[]{:S(2)}) async-start(bf16[56,1,16,384]{3,0,1,2:T(8,128)(2,1)} %bitcast.61), calls=%async_computation | async-start | bytes 1376256 | tf_op jit(solution)/shard_map/all_to_all | solution.py:44
  206.1 0.1 copy.52
  206.5 1.2 reduce-window.6
  207.6 0.2 slice_reduce_fusion
  208.2 0.1 copy.60
  208.4 0.7 copy.56
  209.1 0.9 dynamic-slice_convert_fusion
  210.1 0.1 mul.43
  210.2 0.3 mul.44
  210.5 0.5 fusion.18
  211.0 0.6 exponential_reduce_fusion
  211.6 19.9 %all-to-all-done = bf16[56,1,16,384]{3,0,1,2:T(8,128)(2,1)} async-done(((bf16[56,1,16,384]{3,0,1,2:T(8,128)(2,1)}), bf16[56,1,16,384]{3,0,1,2:T(8,128)(2,1)}, u32[]{:S(2)}, u32[]{:S(2)}) %all-to-all-start) | async-done | bytes 688160 | tf_op jit(solution)/shard_map/all_to_all | solution.py:44
  231.6 1.2 copy.59
  232.7 1.9 gather_fusion
  234.8 1.6 fusion.5
  236.5 0.1 copy.61
  236.7 2.7 scatter_custom_fusion
  239.4 1.0 copy.62
  240.4 5.4 all-to-all-start.1
  245.9 0.2 copy.64
  246.1 1.5 convolution_bitcast_fusion
  247.6 0.5 fusion.6
  248.1 0.7 copy.77
  248.8 501.9 %all-reduce.2.cloned.1.call-done = f32[6144,16]{0,1:T(8,128)} async-done(((f32[6144,16]{0,1:T(8,128)}), f32[6144,16]{0,1:T(8,128)}) %all-reduce.2.cloned.1.call-update) | async-done | bytes 393232 | tf_op jit(solution)/shard_map/psum | solution.py:56
  750.6 1.8 broadcast_multiply_fusion
  752.4 0.9 copy.63
  (39 shorter events, 1.2 us)
Async XLA Ops:
  7.2 203.3 %copy-start = (bf16[128,6144]{1,0:T(8,128)(2,1)S(1)}, bf16[128,6144]{1,0:T(8,128)(2,1)}, u32[]{:S(2)}) copy-start(bf16[128,6144]{1,0:T(8,128)(2,1)} %param.6) | copy-start | bytes 4718596
  7.2 184.9 %reduce-scatter.4.cloned.1.call-start = ((), (), s32[]{:S(2)}) async-start(), calls=%async_computation.4 | async-start | bytes 6193152
  195.8 10.3 %copy-start.4 = (s32[128,4]{0,1:T(4,128)S(1)}, s32[128,4]{0,1:T(4,128)}, u32[]{:S(2)}) copy-start(s32[128,4]{0,1:T(4,128)} %param.10) | copy-start | bytes 6148
  197.6 33.9 %all-to-all-start = ((bf16[56,1,16,384]{3,0,1,2:T(8,128)(2,1)}), bf16[56,1,16,384]{3,0,1,2:T(8,128)(2,1)}, u32[]{:S(2)}, u32[]{:S(2)}) async-start(bf16[56,1,16,384]{3,0,1,2:T(8,128)(2,1)} %bitcast.61), calls=%async_computation | async-start | bytes 1376256 | tf_op jit(solution)/shard_map/all_to_all | solution.py:44
  208.2 2.3 copy-start.3
  234.8 1.8 copy-start.1
  234.8 1.6 copy-start.6
  240.4 512.0 %all-to-all-start.1 = ((bf16[56,16,1,384]{3,0,2,1:T(8,128)(2,1)}), bf16[56,16,1,384]{3,0,2,1:T(8,128)(2,1)S(1)}, u32[]{:S(2)}, u32[]{:S(2)}) async-start(bf16[56,16,1,384]{3,0,2,1:T(8,128)(2,1)} %copy.62), calls=%async_computation.1 | async-start | bytes 1376256 | tf_op jit(solution)/shard_map/all_to_all | solution.py:64
  245.8 1.8 copy-start.2
  245.8 1.8 copy-start.5
  245.8 504.8 %all-reduce.2.cloned.1.call-start = ((), (), s32[]{:S(2)}) async-start(), calls=%async_computation.3 | async-start | bytes 786432 | tf_op jit(solution)/shard_map/psum | solution.py:56
Sparse Core Ops, SparseCore 0:
  51.3 140.6 reduce-scatter.3
  252.1 498.4 all-reduce.1
where the time goes:
time: 763 us; the launch traced here: 760 us
  waiting for transfers between devices  663 us (87%)
  local copies, waits for them, and re-layouts  48.4 us (6%)
  between operations  14.3 us (2%)
  starting transfers between devices  14 us (2%)
  matrix products  13.5 us (2%)
    psum x1, waiting for transfers between devices, per_device(): router_total = lax.psum(partial_router, ('dp', 'ctx', 'tp'))  502 us
    unnamed x3, waiting for transfers between devices  141 us
    unnamed x20, local copies, waits for them, and re-layouts  41.1 us
    all_to_all x1, waiting for transfers between devices, per_device(): lax.all_to_all(summed, 'ctx', split_axis=2, concat_axis=1, tiled=True)  19.9 us
  transfers between devices with their start and end apart: 4, of which 3 were waited for; matrix products, arithmetic and copies ran while one was open for 1% of the time, Pallas kernels for 0%

commit v1 on v0

--- a/solution.py
+++ b/solution.py
@@ -1,18 +1,130 @@
 import jax
 import jax.numpy as jnp
 from jax import lax
+from jax.experimental import pallas as pl
+from jax.experimental.pallas import tpu as pltpu
 from jax.sharding import PartitionSpec as P
 
-
-def round_term(values):
-    rounded = lax.optimization_barrier(values.astype(jnp.bfloat16))
-    return rounded.astype(jnp.float32)
+MESH = pl.DeviceIdType.MESH
 
 
-def spread_grad(gate_values, gate_grad, onehot):
-    mix_term = jnp.sum(gate_values * gate_grad, axis=1, keepdims=True)
-    chosen_grad = gate_values * (gate_grad - mix_term)
-    return jnp.sum(jnp.where(onehot, chosen_grad[:, :, None], 0.0), axis=1)
+def router_kernel(
+    gg_ref, gate_ref, tok_ref, out_ref,
+    gg_all, tok_cols, part, from_dp, from_ctx, tok_sem,
+    send0, recv0, send1, recv1, send2, recv2, send3, recv3, send4, recv4,
+):
+    dp, ctx, tp = lax.axis_index("dp"), lax.axis_index("ctx"), lax.axis_index("tp")
+    n_dp, n_ctx, n_tp = lax.axis_size("dp"), lax.axis_size("ctx"), lax.axis_size("tp")
+    width = tok_cols.shape[1]
+    columns = pl.ds(pl.multiple_of(tp * width, 128), width)
+    load = pltpu.make_async_copy(tok_ref.at[:, columns], tok_cols, tok_sem)
+    load.start()
+
+    def at_dp(k):
+        return (lax.rem(dp + k, n_dp), ctx, tp)
+
+    def at_ctx(k):
+        return (dp, lax.rem(ctx + k, n_ctx), tp)
+
+    def at_tp(k):
+        return (dp, ctx, lax.rem(tp + k, n_tp))
+
+    barrier = pltpu.get_barrier_semaphore()
+    for count, where in ((n_tp, at_tp), (n_dp, at_dp), (n_ctx, at_ctx)):
+        @pl.loop(1, count)
+        def _(k):
+            pl.semaphore_signal(barrier, inc=1, device_id=where(k), device_id_type=MESH)
+    pl.semaphore_wait(barrier, n_tp + n_dp + n_ctx - 3)
+
+    def exchange(count, me, where, source, target, send, recv):
+        def copy(k, slot):
+            return pltpu.make_async_remote_copy(
+                src_ref=source(lax.rem(me + k, count)),
+                dst_ref=target(slot),
+                send_sem=send.at[lax.rem(me + k, count)],
+                recv_sem=recv.at[slot],
+                device_id=where(k),
+                device_id_type=MESH,
+            )
+
+        @pl.loop(1, count)
+        def _(k):
+            copy(k, me).start()
+
+        @pl.loop(1, count)
+        def _(k):
+            copy(k, lax.rem(me + k, count)).wait_recv()
+
+        @pl.loop(1, count)
+        def _(k):
+            copy(k, me).wait_send()
+
+    gg_all[tp] = gg_ref[...]
+    exchange(n_tp, tp, at_tp, lambda k: gg_ref, lambda k: gg_all.at[k], send0, recv0)
+    gate_grad = gg_all[0]
+    for k in range(1, n_tp):
+        gate_grad = gate_grad + gg_all[k]
+    gates = gate_ref[...]
+    mix_term = jnp.sum(gates * gate_grad, axis=0, keepdims=True)
+    logit_grad = gates * (gate_grad - mix_term)
+    high = logit_grad.astype(jnp.bfloat16)
+    rest = logit_grad - high.astype(jnp.float32)
+    middle = rest.astype(jnp.bfloat16)
+    low = (rest - middle.astype(jnp.float32)).astype(jnp.bfloat16)
+    load.wait()
+    token_cols = tok_cols[...]
+    product = jnp.dot(low, token_cols, preferred_element_type=jnp.float32)
+    product += jnp.dot(middle, token_cols, preferred_element_type=jnp.float32)
+    product += jnp.dot(high, token_cols, preferred_element_type=jnp.float32)
+    product = product * (1.0 / tok_cols.shape[0])
+    experts = product.shape[0]
+    each, lanes = experts // n_dp, width // 128
+    for e in range(experts):
+        for k in range(lanes):
+            row = (e % each) * lanes + k
+            part[e // each, row // 4, row % 4 : row % 4 + 1, :] = product[e : e + 1, k * 128 : (k + 1) * 128]
+
+    from_dp[dp] = part[dp]
+    exchange(n_dp, dp, at_dp, lambda k: part.at[k], lambda k: from_dp.at[k], send1, recv1)
+    total = from_dp[0]
+    for k in range(1, n_dp):
+        total = total + from_dp[k]
+    from_ctx[ctx] = total
+    exchange(n_ctx, ctx, at_ctx, lambda k: from_ctx.at[ctx], lambda k: from_ctx.at[k], send2, recv2)
+    total = from_ctx[0]
+    for k in range(1, n_ctx):
+        total = total + from_ctx[k]
+    out_ref[dp, tp] = total
+    exchange(n_tp, tp, at_tp, lambda k: out_ref.at[dp, tp], lambda k: out_ref.at[dp, k], send3, recv3)
+    exchange(n_dp, dp, at_dp, lambda k: out_ref.at[dp], lambda k: out_ref.at[k], send4, recv4)
+
+
+def router_sum(gate_part, gates, tokens):
+    n_dp, n_ctx, n_tp = lax.axis_size("dp"), lax.axis_size("ctx"), lax.axis_size("tp")
+    experts, tok_count = gates.shape
+    width = tokens.shape[1] // n_tp
+    each, lanes = experts // n_dp, width // 128
+    chunk = (each * lanes // 4, 4, 128)
+    vmem = pl.BlockSpec(memory_space=pltpu.VMEM)
+    sems = [pltpu.SemaphoreType.DMA((n,)) for n in (n_tp, n_tp, n_dp, n_dp, n_ctx, n_ctx, n_tp, n_tp, n_dp, n_dp)]
+    gathered = pl.pallas_call(
+        router_kernel,
+        out_shape=jax.ShapeDtypeStruct((n_dp, n_tp) + chunk, jnp.float32),
+        in_specs=[vmem, vmem, pl.BlockSpec(memory_space=pl.ANY)],
+        out_specs=vmem,
+        scratch_shapes=[
+            pltpu.VMEM((n_tp, experts, tok_count), jnp.float32),
+            pltpu.VMEM((tok_count, width), jnp.bfloat16),
+            pltpu.VMEM((n_dp,) + chunk, jnp.float32),
+            pltpu.VMEM((n_dp,) + chunk, jnp.float32),
+            pltpu.VMEM((n_ctx,) + chunk, jnp.float32),
+            pltpu.SemaphoreType.DMA,
+        ] + sems,
+        compiler_params=pltpu.CompilerParams(collective_id=1, has_side_effects=True, vmem_limit_bytes=16 << 20),
+        name="router_sum",
+    )(gate_part, gates, tokens)
+    gathered = gathered.reshape(n_dp, n_tp, each, lanes, 128)
+    return gathered.transpose(1, 3, 4, 0, 2).reshape(tokens.shape[1], experts)
 
 
 def per_device(tokens, router_weight, expert_hidden, down_weight, expert_ids, mixed_grad):
@@ -36,11 +148,10 @@
     route_index = (slot_index * experts_all + expert_ids).reshape(-1)
     grad_cols = lax.dynamic_slice_in_dim(mixed_grad, tp_index * col_width, col_width, 1)
     partial_sum = jnp.einsum(
-        "cesf,efd->cesd", hidden, down_weight, preferred_element_type=jnp.float32
-    )
-    summed = lax.psum_scatter(
-        round_term(partial_sum).astype(jnp.bfloat16), "tp", scatter_dimension=3, tiled=True
-    )
+        "fd,rf->dr", down_weight[0], hidden.reshape(-1, hidden.shape[-1]), preferred_element_type=jnp.float32
+    ).astype(jnp.bfloat16)
+    summed = lax.psum_scatter(partial_sum, "tp", scatter_dimension=0, tiled=True)
+    summed = summed.T.reshape(capacity, 1, experts_all, col_width)
     arrived = lax.all_to_all(summed, "ctx", split_axis=2, concat_axis=1, tiled=True)
     row_table = arrived.reshape(capacity * experts_all, col_width)
     picked = (
@@ -50,11 +161,9 @@
     )
     combined = jnp.einsum("tk,tkd->td", gate_values, picked).astype(jnp.bfloat16)
     gate_part = jnp.einsum("tkd,td->tk", picked, grad_cols.astype(jnp.float32))
-    token_wide = tokens.astype(jnp.float32)
-    logit_grad = spread_grad(gate_values, gate_part, onehot)
-    partial_router = jnp.dot(token_wide.T, logit_grad, precision=lax.Precision.HIGHEST)
-    router_total = lax.psum(partial_router, ("dp", "ctx", "tp"))
-    router_grad = router_total / tok_count
+    gate_map = jnp.sum(jnp.where(onehot, gate_values[:, :, None], 0.0), axis=1).T
+    part_map = jnp.sum(jnp.where(onehot, gate_part[:, :, None], 0.0), axis=1).T
+    router_grad = router_sum(part_map, gate_map, tokens)
     grad_values = (gate_values[:, :, None] * grad_cols[:, None, :].astype(jnp.float32)).astype(
         jnp.bfloat16
     )

time: 763 us -> 304 us (0.40)
  waiting for transfers between devices: 663 us -> 158 us
  Pallas kernels: 0 us -> 60.1 us
  local copies, waits for them, and re-layouts: 48.4 us -> 22.8 us
  starting transfers between devices: 14 us -> 30.2 us
    psum x1 -> x0, waiting for transfers between devices: 502 us -> none  [per_device(): router_total = lax.psum(partial_router, ('dp', 'ctx', 'tp'))]
    unnamed x3 -> x1, waiting for transfers between devices: 141 us -> 0.02 us
    reduce_scatter x0 -> x1, waiting for transfers between devices: none -> 134 us  [per_device(): lax.psum_scatter(partial_sum, 'tp', scatter_dimension=0, tiled=True)]
    pallas_call x0 -> x1, Pallas kernels: none -> 60.1 us  [router_sum(): pl.pallas_call(router_kernel, out_shape=jax.ShapeDtypeStruct((n_dp, n_tp)...]
    unnamed x20 -> x12, local copies, waits for them, and re-layouts: 41.1 us -> 4.11 us
    all_to_all x1, starting transfers between devices: 5.44 us -> 21.7 us  [per_device(): lax.all_to_all(outgoing, 'ctx', split_axis=1, concat_axis=2, tiled=True)]
  transfers between devices with their start and end apart: 4 -> 3, of which waited for: 3 -> 2; matrix products, arithmetic and copies ran while one was open for 1% -> 7% of each run, Pallas kernels for 0% -> 0%
where the time goes in v1:
time: 304 us; the launch traced here: 303 us
  waiting for transfers between devices  158 us (52%)
  Pallas kernels  60.1 us (20%)
  starting transfers between devices  30.2 us (10%)
  local copies, waits for them, and re-layouts  22.8 us (8%)
  between operations  14.2 us (5%)
  matrix products  11.8 us (4%)
  other arithmetic  6.42 us (2%)
    reduce_scatter x1, waiting for transfers between devices, per_device(): lax.psum_scatter(partial_sum, 'tp', scatter_dimension=0, tiled=True)  134 us
    pallas_call x1, Pallas kernels, router_sum(): pl.pallas_call(router_kernel, out_shape=jax.ShapeDtypeStruct((n_dp, n_tp)...  60.1 us
    all_to_all x1, waiting for transfers between devices, per_device(): lax.all_to_all(summed, 'ctx', split_axis=2, concat_axis=1, tiled=True)  23.4 us
    all_to_all x1, starting transfers between devices, per_device(): lax.all_to_all(outgoing, 'ctx', split_axis=1, concat_axis=2, tiled=True)  21.7 us
    dot_general x1, matrix products, per_device(): jnp.einsum('fd,rf->dr', down_weight[0], hidden.reshape(-1, hidden.shape[-...  9.03 us
    all_to_all x1, starting transfers between devices, per_device(): lax.all_to_all(summed, 'ctx', split_axis=2, concat_axis=1, tiled=True)  8.47 us
  transfers between devices with their start and end apart: 3, of which 2 were waited for; matrix products, arithmetic and copies ran while one was open for 7% of the time, Pallas kernels for 0%

profile of v1, /device:TPU:6, one launch (start us, length us, event | category | flops | bytes accessed | tf_op | source)
XLA Modules:
  0.0 303.1 jit_solution(7013997312533063099)
XLA Ops:
  7.2 1.3 copy-done
  8.5 9.0 %convolution_convert_fusion = bf16[3072,896]{1,0:T(8,128)(2,1)} fusion(bf16[896,672]{1,0:T(8,128)(2,1)S(1)} %bitcast.48, bf16[1,672,3072]{2,1,0:T(8,128)(2,1)} %param.9), kind=kOutput, calls=%fused_computation.2 | convolution fusion | flops 3702128640 | bytes 10838016 | tf_op jit(solution)/shard_map/fd,rf->dr/dot_general | solution.py:150
  17.6 0.7 copy-done.4
  18.2 0.1 copy.60
  18.6 1.2 reduce-window.6
  19.7 0.2 slice_reduce_fusion
  20.3 0.1 copy.68
  20.4 0.1 reshape.124
  20.6 1.1 dynamic-slice_bitcast_fusion
  21.6 1.1 mul.37
  22.7 2.3 mul.38
  25.0 0.5 fusion.15
  25.6 0.1 copy.69
  25.8 3.9 %scatter_custom_fusion = bf16[896,384]{1,0:T(8,128)(2,1)} fusion(s32[512]{0:T(512)S(1)} %bitcast.57, f32[512,384]{1,0:T(8,128)} %mul.38, f32[512]{0:T(512)S(1)} %div.18, bf16[]{:T(256)} %constant.17.clone.1), kind=kCustom, calls=%fused_computation.5 | custom fusion | flops 393216 | bytes 1476610 | tf_op jit(solution)/shard_map/scatter | solution.py:171
  29.7 2.1 copy.70
  31.8 21.7 %all-to-all-start.1 = ((bf16[56,16,1,384]{3,0,2,1:T(8,128)(2,1)}), bf16[56,16,1,384]{3,0,2,1:T(8,128)(2,1)}, u32[]{:S(2)}, u32[]{:S(2)}) async-start(bf16[56,16,1,384]{3,0,2,1:T(8,128)(2,1)} %copy.70), calls=%async_computation.2 | async-start | bytes 1376256 | tf_op jit(solution)/shard_map/all_to_all | solution.py:173
  53.5 134.2 %reduce-scatter.2.cloned.1.call-done = bf16[384,896]{1,0:T(8,128)(2,1)} async-done(((bf16[3072,896]{1,0:T(8,128)(2,1)}), bf16[384,896]{1,0:T(8,128)(2,1)}) %reduce-scatter.2.cloned.1.call-update) | async-done | bytes 688144 | tf_op jit(solution)/shard_map/reduce_scatter | solution.py:153
  187.7 2.2 copy.65
  189.9 2.1 copy.66
  192.0 8.5 %all-to-all-start = ((bf16[56,1,16,384]{3,0,1,2:T(8,128)(2,1)}), bf16[56,1,16,384]{3,0,1,2:T(8,128)(2,1)}, u32[]{:S(2)}, u32[]{:S(2)}) async-start(bf16[56,1,16,384]{3,0,1,2:T(8,128)(2,1)} %copy.66), calls=%async_computation.1 | async-start | bytes 1376256 | tf_op jit(solution)/shard_map/all_to_all | solution.py:155
  200.5 0.1 copy.64
  200.6 0.2 copy.74
  200.8 2.0 copy.73
  202.8 23.4 %all-to-all-done = bf16[56,1,16,384]{3,0,1,2:T(8,128)(2,1)} async-done(((bf16[56,1,16,384]{3,0,1,2:T(8,128)(2,1)}), bf16[56,1,16,384]{3,0,1,2:T(8,128)(2,1)}, u32[]{:S(2)}, u32[]{:S(2)}) %all-to-all-start) | async-done | bytes 688160 | tf_op jit(solution)/shard_map/all_to_all | solution.py:155
  226.3 2.0 copy.67
  228.3 3.0 gather_fusion
  231.3 0.8 gather.7
  232.1 1.8 fusion.4
  234.0 60.1 %router_sum.1 = f32[8,8,3,4,128]{4,3,2,1,0:T(4,128)S(1)} custom-call(f32[16,128]{1,0:T(8,128)S(1)} %bitcast.50, f32[16,128]{1,0:T(8,128)S(1)} %bitcast.49, bf16[128,6144]{1,0:T(8,128)(2,1)S(1)} %copy-done.1), custom_call_target="tpu_custom_call" | custom-call | tf_op jit(solution)/shard_map/router_sum/pallas_call | solution.py:110
  294.3 0.9 reshape.127
  295.1 0.5 fusion.5
  295.6 0.7 copy.83
  (32 shorter events, 1.0 us)
Async XLA Ops:
  7.2 1.3 copy-start
  7.2 180.5 %reduce-scatter.2.cloned.1.call-start = ((), (), s32[]{:S(2)}) async-start(), calls=%async_computation.3 | async-start | bytes 6193152 | tf_op jit(solution)/shard_map/reduce_scatter | solution.py:153
  17.5 0.7 copy-start.4
  20.2 4.8 %copy-start.1 = (bf16[128,6144]{1,0:T(8,128)(2,1)S(1)}, bf16[128,6144]{1,0:T(8,128)(2,1)}, u32[]{:S(2)}) copy-start(bf16[128,6144]{1,0:T(8,128)(2,1)} %tok_ref.1) | copy-start | bytes 4718596
  20.2 4.8 %copy-start.3 = (bf16[6144,16]{0,1:T(8,128)(2,1)S(1)}, bf16[6144,16]{0,1:T(8,128)(2,1)}, u32[]{:S(2)}) copy-start(bf16[6144,16]{0,1:T(8,128)(2,1)} %param.7) | copy-start | bytes 589828
  31.8 160.2 %all-to-all-start.1 = ((bf16[56,16,1,384]{3,0,2,1:T(8,128)(2,1)}), bf16[56,16,1,384]{3,0,2,1:T(8,128)(2,1)}, u32[]{:S(2)}, u32[]{:S(2)}) async-start(bf16[56,16,1,384]{3,0,2,1:T(8,128)(2,1)} %copy.70), calls=%async_computation.2 | async-start | bytes 1376256 | tf_op jit(solution)/shard_map/all_to_all | solution.py:173
  192.0 34.3 %all-to-all-start = ((bf16[56,1,16,384]{3,0,1,2:T(8,128)(2,1)}), bf16[56,1,16,384]{3,0,1,2:T(8,128)(2,1)}, u32[]{:S(2)}, u32[]{:S(2)}) async-start(bf16[56,1,16,384]{3,0,1,2:T(8,128)(2,1)} %copy.66), calls=%async_computation.1 | async-start | bytes 1376256 | tf_op jit(solution)/shard_map/all_to_all | solution.py:155
  294.1 1.0 copy-start.2
Sparse Core Ops, SparseCore 0:
  17.7 169.9 reduce-scatter.1

commit v2 on v0

v2 whole, which is shorter than its diff:
```python
import jax
import jax.numpy as jnp
from jax import lax
from jax.experimental import pallas as pl
from jax.experimental.pallas import tpu as pltpu
from jax.sharding import PartitionSpec as P

MESH = pl.DeviceIdType.MESH
AHEAD = 3


def layer_kernel(
    rows_ref, weight_ref, grad_ref, info_ref, gate_ref, tok_ref,
    comb_ref, slot_grad_ref, router_ref,
    weight, grads, tok_cols, made, arrived, passed_in, passed_out, mix, chosen, dots, total,
    info, gg_out, gg_all, comb_out, comb_in, grad_out, part, from_dp, from_ctx,
    load_sem, tok_sem, weight_sem, x_send, x_recv, z_send, z_recv, mg_send, mg_recv,
    pair_send, pair_recv, rg_send, rg_recv, gg_send, gg_recv,
    send1, recv1, send2, recv2, send3, recv3, send4, recv4,
):
    dp, ctx, z = lax.axis_index("dp"), lax.axis_index("ctx"), lax.axis_index("tp")
    n_dp, n_ctx, n_z = lax.axis_size("dp"), lax.axis_size("ctx"), lax.axis_size("tp")
    n_q = n_ctx // 2
    half, q = ctx // n_q, lax.rem(ctx, n_q)
    last = n_z - 1
    cols = grads.shape[2]
    toks = grad_ref.shape[0]
    own_rows = pl.ds(pl.multiple_of(half * toks, toks), toks)
    other_rows = pl.ds(pl.multiple_of((1 - half) * toks, toks), toks)

    def at_dp(k):
        return (lax.rem(dp + k, n_dp), ctx, z)

    def at_ctx(k):
        return (dp, lax.rem(ctx + k, n_ctx), z)

    def at_z(k):
        return (dp, ctx, lax.rem(z + k, n_z))

    def at_q(k):
        return (dp, half * n_q + lax.rem(q + k, n_q), z)

    def remote(src, dst, send, recv, device):
        return pltpu.make_async_remote_copy(
            src_ref=src, dst_ref=dst, send_sem=send, recv_sem=recv, device_id=device, device_id_type=MESH
        )

    pair = (dp, (1 - half) * n_q + q, z)
    upper = (dp, ctx, jnp.minimum(z + 1, last))
    lower = (dp, ctx, jnp.maximum(z - 1, 0))

    flip = z // (n_z // 2)
    near = z + flip * (last - 2 * z)

    def block_at(n):
        later = n - (last - 2 * near)
        reach = near - later // 2
        inner = near + reach - 2 * reach * lax.rem(later + 2 * n_z, 2)
        block = jnp.where(later < 0, last - n, inner)
        return block + flip * (last - 2 * block)

    width = tok_cols.shape[1]
    tok_load = pltpu.make_async_copy(
        tok_ref.at[:, pl.ds(pl.multiple_of(z * width, 128), width)], tok_cols, tok_sem
    )
    tok_load.start()

    def weight_load(b):
        return pltpu.make_async_copy(
            weight_ref.at[:, pl.ds(pl.multiple_of(b * cols, 128), cols)], weight.at[b], weight_sem.at[b]
        )

    def grad_load(b):
        return pltpu.make_async_copy(
            grad_ref.at[:, pl.ds(pl.multiple_of(b * cols, 128), cols)], grads.at[b, own_rows], load_sem.at[b]
        )

    @pl.loop(0, n_z)
    def _(n):
        weight_load(block_at(n)).start()

    @pl.loop(0, n_z)
    def _(b):
        grad_load(b).start()

    barrier = pltpu.get_barrier_semaphore()
    for count, where in ((n_z, at_z), (n_dp, at_dp), (n_ctx, at_ctx)):
        @pl.loop(1, count)
        def _(k):
            pl.semaphore_signal(barrier, inc=1, device_id=where(k), device_id_type=MESH)

    @pl.loop(1, n_z)
    def _(k):
        there = (dp, (1 - half) * n_q + q, lax.rem(z + k, n_z))
        pl.semaphore_signal(barrier, inc=1, device_id=there, device_id_type=MESH)

    @pl.loop(0, n_z)
    def _(b):
        grad_load(b).wait()

    pl.semaphore_wait(barrier, 2 * n_z + n_dp + n_ctx - 4)

    info[half] = info_ref[half]
    pair_info = remote(info_ref.at[1 - half], info.at[half], pair_send.at[0], pair_recv.at[0], pair)
    pair_grad = remote(grads.at[z, own_rows], grads.at[z, own_rows], pair_send.at[1], pair_recv.at[1], pair)
    got_info = remote(info_ref.at[half], info.at[1 - half], pair_send.at[0], pair_recv.at[0], pair)
    got_grad = remote(grads.at[z, other_rows], grads.at[z, other_rows], pair_send.at[1], pair_recv.at[1], pair)
    pair_info.start()
    pair_grad.start()

    def x_copy(b, k):
        to = lax.rem(q + k, n_q)
        return remote(made.at[b, to], arrived.at[b, q], x_send.at[b, to], x_recv.at[b, q], at_q(k))

    def x_wait(b, k):
        come = lax.rem(q + k, n_q)
        return remote(made.at[b, come], arrived.at[b, come], x_send.at[b, come], x_recv.at[b, come], at_q(k))

    def produce(n):
        b = block_at(n)
        weight_load(b).wait()

        @pl.loop(0, n_q // 2)
        def _(r):
            rows = rows_ref[pl.ds(2 * r, 2)]
            size = rows.shape[1]
            product = jnp.dot(
                rows.reshape(2 * size, rows.shape[2]), weight[b], preferred_element_type=jnp.float32
            )
            made[b, pl.ds(2 * r, 2)] = product.astype(jnp.bfloat16).reshape(2, size, cols)

        @pl.loop(1, n_q)
        def _(k):
            x_copy(b, k).start()

        arrived[b, q] = made[b, q]

    for n in range(AHEAD):
        produce(n)

    got_info.wait_recv()
    per_q = rows_ref.shape[1]
    experts_here = n_q

    def chosen_mask():
        code = jnp.concatenate([info[0, 1], info[1, 1]], axis=1)
        spot = lax.broadcasted_iota(jnp.int32, (experts_here, per_q, 2 * toks), 1).astype(jnp.float32)
        return jnp.broadcast_to(code[:, None, :], spot.shape) == spot

    mask = chosen_mask()
    gate = jnp.concatenate([info[0, 0], info[1, 0]], axis=1)
    spread = jnp.where(mask, jnp.broadcast_to(gate[:, None, :], mask.shape), 0.0)
    spread = spread.reshape(experts_here * per_q, 2 * toks)
    chosen[...] = jnp.where(mask, 1.0, 0.0).reshape(spread.shape).astype(jnp.bfloat16)
    turned = spread.T
    high = turned.astype(jnp.bfloat16)
    mix[0] = high
    mix[1] = (turned - high.astype(jnp.float32)).astype(jnp.bfloat16)
    row_gate = jnp.sum(spread, axis=1, keepdims=True)
    dots[...] = jnp.zeros(dots.shape, jnp.float32)

    got_grad.wait_recv()
    picked_grad = jnp.dot(chosen[...], grads[z], preferred_element_type=jnp.float32) * row_gate
    grad_out[...] = picked_grad.astype(jnp.bfloat16).reshape(grad_out.shape)
    slot_grad_ref[q] = grad_out[q]

    def rg_copy(k):
        to = lax.rem(q + k, n_q)
        return remote(grad_out.at[to], slot_grad_ref.at[q], rg_send.at[to], rg_recv.at[q], at_q(k))

    def rg_wait(k):
        come = lax.rem(q + k, n_q)
        return remote(grad_out.at[come], slot_grad_ref.at[come], rg_send.at[come], rg_recv.at[come], at_q(k))

    @pl.loop(1, n_q)
    def _(k):
        rg_copy(k).start()

    def mg_copy(b, device):
        here = grads.at[b, other_rows]
        return remote(here, here, mg_send.at[b], mg_recv.at[b], device)

    def mg_copy_low(b, device):
        here = grads.at[b, other_rows]
        return remote(here, here, mg_send.at[n_z + b], mg_recv.at[b], device)

    def mg_step(j):
        below, above = z - j, z + j

        @pl.when((j > 0) & (below >= 0))
        def _():
            mg_copy(below, lower).wait_recv()

        @pl.when((j > 0) & (above <= last))
        def _():
            mg_copy(above, upper).wait_recv()

        @pl.when((below >= 0) & (z < last))
        def _():
            mg_copy(below, upper).start()

        @pl.when((above <= last) & (z > 0))
        def _():
            mg_copy_low(above, lower).start()

    def mg_finish(j):
        below, above = z - j, z + j

        @pl.when((below >= 0) & (z < last))
        def _():
            mg_copy(below, upper).wait_send()

        @pl.when((above <= last) & (z > 0))
        def _():
            mg_copy_low(above, lower).wait_send()

    def mixed(b):
        rows = arrived[b].reshape(n_q * per_q, cols)
        return jnp.dot(mix[0], rows, preferred_element_type=jnp.float32) + jnp.dot(
            mix[1], rows, preferred_element_type=jnp.float32
        )

    def add_dots(b):
        rows = arrived[b].reshape(n_q * per_q, cols)
        dots[...] += lax.dot_general(
            rows, grads[b], (((1,), (1,)), ((), ())), preferred_element_type=jnp.float32
        )

    def z_copy(b, slot, device):
        return remote(passed_out.at[b], passed_in.at[slot], z_send.at[b], z_recv.at[slot], device)

    def x_wait_all(b):
        @pl.loop(1, n_q)
        def _(k):
            x_wait(b, k).wait_recv()

    @pl.loop(0, last)
    def _(n):
        b = block_at(n)
        x_wait_all(b)

        @pl.when(n + AHEAD < n_z)
        def _():
            produce(n + AHEAD)

        @pl.when(n < n_z // 2)
        def _():
            mg_step(2 * n)
            mg_step(2 * n + 1)

        total[...] = mixed(b)
        up = b > z

        @pl.when((up & (z > 0)) | (jnp.logical_not(up) & (z < last)))
        def _():
            z_copy(b, b, lower).wait_recv()
            total[...] += passed_in[b].astype(jnp.float32)

        passed_out[b] = total[...].astype(jnp.bfloat16)

        @pl.when(up)
        def _():
            z_copy(b, b, upper).start()

        @pl.when(b < z - 1)
        def _():
            z_copy(b, b, lower).start()

        @pl.when(b == z - 1)
        def _():
            z_copy(b, n_z, lower).start()

        @pl.when(n == n_z // 2)
        def _():
            @pl.loop(0, n_z // 2)
            def _(m):
                add_dots(block_at(m))

        @pl.when(n >= n_z // 2)
        def _():
            add_dots(b)

    x_wait_all(z)
    add_dots(z)
    gate_grad = jnp.where(chosen_mask(), dots[...].reshape(experts_here, per_q, 2 * toks), 0.0)
    gate_grad = jnp.sum(gate_grad, axis=1)
    gg_out[0] = gate_grad[:, :toks]
    gg_out[1] = gate_grad[:, toks:]
    gg_all[half * n_z + z] = gg_out[half]
    spot = half * n_z + z

    def gg_copy(k, slot):
        to = lax.rem(spot + k, 2 * n_z)
        to_half = to // n_z
        return remote(
            gg_out.at[to_half], gg_all.at[slot], gg_send.at[to], gg_recv.at[slot],
            (dp, to_half * n_q + q, lax.rem(to, n_z)),
        )

    @pl.loop(1, 2 * n_z)
    def _(k):
        gg_copy(k, spot).start()

    total[...] = mixed(z)

    @pl.when(z > 0)
    def _():
        z_copy(z, z, lower).wait_recv()
        total[...] += passed_in[z].astype(jnp.float32)

    @pl.when(z < last)
    def _():
        z_copy(z, n_z, upper).wait_recv()
        total[...] += passed_in[n_z].astype(jnp.float32)

    comb_out[...] = total[other_rows, :].astype(jnp.bfloat16)
    pair_comb = remote(comb_out, comb_in, pair_send.at[2], pair_recv.at[2], pair)
    pair_comb.start()

    @pl.loop(1, 2 * n_z)
    def _(k):
        gg_copy(k, lax.rem(spot + k, 2 * n_z)).wait_recv()

    parts = []
    for h in range(2):
        summed = gg_all[h * n_z]
        for k in range(1, n_z):
            summed = summed + gg_all[h * n_z + k]
        parts.append(summed)
    gate_grad = jnp.concatenate(parts, axis=0)
    gates = gate_ref[...]
    mix_term = jnp.sum(gates * gate_grad, axis=0, keepdims=True)
    logit_grad = gates * (gate_grad - mix_term)
    high = logit_grad.astype(jnp.bfloat16)
    rest = logit_grad - high.astype(jnp.float32)
    middle = rest.astype(jnp.bfloat16)
    low = (rest - middle.astype(jnp.float32)).astype(jnp.bfloat16)
    tok_load.wait()
    token_cols = tok_cols[...]
    product = jnp.dot(low, token_cols, preferred_element_type=jnp.float32)
    product += jnp.dot(middle, token_cols, preferred_element_type=jnp.float32)
    product += jnp.dot(high, token_cols, preferred_element_type=jnp.float32)
    product = product * (1.0 / toks)
    experts = product.shape[0]
    each, lanes = experts // n_dp, width // 128
    for e in range(experts):
        for k in range(lanes):
            row = (e % each) * lanes + k
            part[e // each, row // 4, row % 4 : row % 4 + 1, :] = product[e : e + 1, k * 128 : (k + 1) * 128]

    def exchange(count, me, where, source, target, send, recv):
        def copy(k, slot):
            to = lax.rem(me + k, count)
            return remote(source(to), target(slot), send.at[to], recv.at[slot], where(k))

        @pl.loop(1, count)
        def _(k):
            copy(k, me).start()

        @pl.loop(1, count)
        def _(k):
            copy(k, lax.rem(me + k, count)).wait_recv()

        @pl.loop(1, count)
        def _(k):
            copy(k, me).wait_send()

    from_dp[dp] = part[dp]
    exchange(n_dp, dp, at_dp, lambda k: part.at[k], lambda k: from_dp.at[k], send1, recv1)
    summed = from_dp[0]
    for k in range(1, n_dp):
        summed = summed + from_dp[k]
    from_ctx[ctx] = summed
    exchange(n_ctx, ctx, at_ctx, lambda k: from_ctx.at[ctx], lambda k: from_ctx.at[k], send2, recv2)
    summed = from_ctx[0]
    for k in range(1, n_ctx):
        summed = summed + from_ctx[k]
    router_ref[dp, z] = summed
    exchange(n_z, z, at_z, lambda k: router_ref.at[dp, z], lambda k: router_ref.at[dp, k], send3, recv3)
    exchange(n_dp, dp, at_dp, lambda k: router_ref.at[dp], lambda k: router_ref.at[k], send4, recv4)

    remote(comb_out, comb_in, pair_send.at[2], pair_recv.at[2], pair).wait_recv()
    comb_ref[...] = (total[own_rows, :] + comb_in[...].astype(jnp.float32)).astype(jnp.bfloat16)

    @pl.loop(1, n_q)
    def _(k):
        rg_wait(k).wait_recv()

    pair_info.wait_send()
    pair_grad.wait_send()
    pair_comb.wait_send()

    @pl.loop(1, n_q)
    def _(k):
        rg_copy(k).wait_send()

    @pl.loop(1, 2 * n_z)
    def _(k):
        gg_copy(k, spot).wait_send()

    @pl.loop(0, n_z)
    def _(j):
        mg_finish(j)

        @pl.loop(1, n_q)
        def _(k):
            x_copy(j, k).wait_send()

        @pl.when(j != z)
        def _():
            z_copy(j, j, lower).wait_send()


def layer(rows, weight, grad, info, gates, tokens):
    n_dp, n_ctx, n_z = lax.axis_size("dp"), lax.axis_size("ctx"), lax.axis_size("tp")
    n_q = n_ctx // 2
    per_q, depth = rows.shape[1:]
    full = weight.shape[1]
    cols = full // n_z
    experts, toks = gates.shape
    width = tokens.shape[1] // n_z
    each, lanes = experts // n_dp, width // 128
    chunk = (each * lanes // 4, 4, 128)
    vmem = pl.BlockSpec(memory_space=pltpu.VMEM)
    anywhere = pl.BlockSpec(memory_space=pl.ANY)
    bf16, f32 = jnp.bfloat16, jnp.float32
    dma = pltpu.SemaphoreType.DMA
    scratch = [
        pltpu.VMEM((n_z, depth, cols), bf16),
        pltpu.VMEM((n_z, 2 * toks, cols), bf16),
        pltpu.VMEM((toks, width), bf16),
        pltpu.VMEM((n_z, n_q, per_q, cols), bf16),
        pltpu.VMEM((n_z, n_q, per_q, cols), bf16),
        pltpu.VMEM((n_z + 1, 2 * toks, cols), bf16),
        pltpu.VMEM((n_z, 2 * toks, cols), bf16),
        pltpu.VMEM((2, 2 * toks, n_q * per_q), bf16),
        pltpu.VMEM((n_q * per_q, 2 * toks), bf16),
        pltpu.VMEM((n_q * per_q, 2 * toks), f32),
        pltpu.VMEM((2 * toks, cols), f32),
        pltpu.VMEM((2, 2, n_q, toks), f32),
        pltpu.VMEM((2, n_q, toks), f32),
        pltpu.VMEM((2 * n_z, n_q, toks), f32),
        pltpu.VMEM((toks, cols), bf16),
        pltpu.VMEM((toks, cols), bf16),
        pltpu.VMEM((n_q, per_q, cols), bf16),
        pltpu.VMEM((n_dp,) + chunk, f32),
        pltpu.VMEM((n_dp,) + chunk, f32),
        pltpu.VMEM((n_ctx,) + chunk, f32),
        dma((n_z,)), dma, dma((n_z,)),
        dma((n_z, n_q)), dma((n_z, n_q)),
        dma((n_z,)), dma((n_z + 1,)),
        dma((2 * n_z,)), dma((n_z,)),
        dma((3,)), dma((3,)),
        dma((n_q,)), dma((n_q,)),
        dma((2 * n_z,)), dma((2 * n_z,)),
        dma((n_dp,)), dma((n_dp,)), dma((n_ctx,)), dma((n_ctx,)),
        dma((n_z,)), dma((n_z,)), dma((n_dp,)), dma((n_dp,)),
    ]
    return pl.pallas_call(
        layer_kernel,
        out_shape=(
            jax.ShapeDtypeStruct((toks, cols), bf16),
            jax.ShapeDtypeStruct((n_q, per_q, cols), bf16),
            jax.ShapeDtypeStruct((n_dp, n_z) + chunk, f32),
        ),
        in_specs=[vmem, anywhere, anywhere, vmem, vmem, anywhere],
        out_specs=(vmem, vmem, vmem),
        scratch_shapes=scratch,
        compiler_params=pltpu.CompilerParams(collective_id=1, has_side_effects=True, vmem_limit_bytes=56 << 20),
        name="layer",
    )(rows, weight, grad, info, gates, tokens)


def per_device(tokens, router_weight, expert_hidden, down_weight, expert_ids, mixed_grad):
    ctx_ranks, tp_ranks, dp_ranks = lax.axis_size("ctx"), lax.axis_size("tp"), lax.axis_size("dp")
    half = lax.axis_index("ctx") // (ctx_ranks // 2)
    hidden = expert_hidden[0, :, 0]
    capacity, sources, depth = hidden.shape
    experts = router_weight.shape[1]
    tok_count = tokens.shape[0]
    group = sources // 2
    rows = hidden.reshape(capacity, 2, group, depth).transpose(2, 1, 0, 3)
    rows = rows.reshape(group, 2 * capacity, depth)

    logits = lax.dot_general(
        router_weight, tokens, (((0,), (1,)), ((), ())), preferred_element_type=jnp.float32
    )
    names = jnp.arange(experts, dtype=jnp.int32)[:, None]
    hit = jnp.any(expert_ids.T[:, None, :] == names[None], axis=0)
    weights = jnp.where(hit, jnp.exp(logits), 0.0)
    gates = weights / jnp.sum(weights, axis=0, keepdims=True)
    place = jnp.arange(tok_count, dtype=jnp.int32)
    earlier = (place[:, None] < place[None, :]).astype(jnp.bfloat16)
    slot = jnp.dot(hit.astype(jnp.bfloat16), earlier, preferred_element_type=jnp.float32)
    code = jnp.where(hit, slot + (half * capacity).astype(jnp.float32), -1.0)
    info = jnp.stack([gates.reshape(2, group, tok_count), code.reshape(2, group, tok_count)], axis=1)

    combined, slot_grads, router = layer(rows, down_weight[0], mixed_grad, info, gates, tokens)
    slot_grads = slot_grads.reshape(group, 2, capacity, slot_grads.shape[-1]).transpose(2, 1, 0, 3)
    row_grads = slot_grads.reshape(1, capacity, 1, sources, slot_grads.shape[-1])
    each = experts // dp_ranks
    router = router.reshape(dp_ranks, tp_ranks, each, -1, 128).transpose(0, 2, 1, 3, 4)
    router_grad = router.reshape(experts, tokens.shape[1]).T
    return (combined, row_grads, router_grad)


def solution(mesh):
    return jax.shard_map(
        per_device,
        mesh=mesh,
        in_specs=(
            P(("dp", "ctx"), None),
            P(),
            P("dp", None, "ctx", None, "tp"),
            P("ctx", "tp", None),
            P(("dp", "ctx"), None),
            P(("dp", "ctx"), None),
        ),
        out_specs=(P(("dp", "ctx"), "tp"), P("dp", None, "ctx", None, "tp"), P()),
        check_vma=False,
    )
```

time: 763 us -> 165 us (0.22)
  waiting for transfers between devices: 663 us -> 0 us
  Pallas kernels: 0 us -> 153 us
  local copies, waits for them, and re-layouts: 48.4 us -> 5.28 us
  starting transfers between devices: 14 us -> 0 us
  between operations: 14.3 us -> 0.71 us
  matrix products: 13.5 us -> 2.08 us
    psum x1 -> x0, waiting for transfers between devices: 502 us -> none  [per_device(): router_total = lax.psum(partial_router, ('dp', 'ctx', 'tp'))]
    pallas_call x0 -> x1, Pallas kernels: none -> 153 us  [layer(): pl.pallas_call(layer_kernel, out_shape=(jax.ShapeDtypeStruct((toks, cols)...]
    unnamed x3 -> x0, waiting for transfers between devices: 141 us -> none
    unnamed x20 -> x9, local copies, waits for them, and re-layouts: 41.1 us -> 0.66 us
    all_to_all x2 -> x0, waiting for transfers between devices: 19.9 us -> none  [the longest x1 19.9 us: per_device(): lax.all_to_all(summed, 'ctx', split_axis=2, concat_axis=1, tiled=True)]
    all_to_all x2 -> x0, starting transfers between devices: 13.9 us -> none  [the longest x1 8.46 us: per_device(): lax.all_to_all(summed, 'ctx', split_axis=2, concat_axis=1, tiled=True)]
    dot_general x5 -> x2, matrix products: 13.5 us -> 2.08 us  [the longest x1 1.94 us: per_device(): lax.dot_general(router_weight, tokens, (((0,), (1,)), ((), ())), preferre...]
  transfers between devices with their start and end apart: 4 -> 0, of which waited for: 3 -> 0; matrix products, arithmetic and copies ran while one was open for 1% -> 0% of each run, Pallas kernels for 0% -> 0%
where the time goes in v2:
time: 165 us; the launch traced here: 163 us
  Pallas kernels  153 us (93%)
  local copies, waits for them, and re-layouts  5.28 us (3%)
  matrix products  2.08 us (1%)
  other arithmetic  2.04 us (1%)
    pallas_call x1, Pallas kernels, layer(): pl.pallas_call(layer_kernel, out_shape=(jax.ShapeDtypeStruct((toks, cols)...  153 us

profile of v2, /device:TPU:6, one launch (start us, length us, event | category | flops | bytes accessed | tf_op | source)
XLA Modules:
  0.0 163.1 jit_solution(1203271866746371687)
XLA Ops:
  0.6 0.0 copy-start
  0.6 0.0 copy-start.1
  0.7 0.8 fusion.3
  1.5 0.1 fusion.1
  1.6 0.0 copy-done
  1.6 1.9 %fusion.4 = (f32[128]{0:T(128)S(1)}, f32[16,128]{1,0:T(8,128)S(1)}) fusion(pred[16,128]{1,0:T(8,128)(4,1)S(1)} %fusion.3, bf16[6144,16]{0,1:T(8,128)(2,1)S(1)} %copy-done, bf16[128,6144]{1,0:T(8,128)(2,1)} %tok_ref.1), kind=kOutput, calls=%fused_computation.11 | convolution fusion | flops 25169792 | bytes 1780224 | tf_op jit(solution)/shard_map/dot_general | solution.py:485
  3.6 0.6 broadcast_divide_fusion.gate_ref
  4.2 0.6 pad_maximum_fusion.info_ref
  4.8 0.0 copy-done.1
  4.8 1.5 copy.20
  6.3 153.0 %layer.1 = (bf16[128,384]{1,0:T(8,128)(2,1)}, bf16[8,112,384]{2,1,0:T(8,128)(2,1)}, f32[8,8,3,4,128]{4,3,2,1,0:T(4,128)}) custom-call(bf16[8,112,672]{2,1,0:T(8,128)(2,1)} %bitcast.25, bf16[672,3072]{1,0:T(8,128)(2,1)} %bitcast.26, bf16[128,3072]{1,0:T(8,128)(2,1)} %grad_ref.1, f32[2,2,8,128]{3,2,1,0:T(8,128)} %pad_maximum_fusion.info_ref, ...), custom_call_target="tpu_custom_call" | custom-call | tf_op jit(solution)/shard_map/layer/pallas_call | solution.py:459
  159.3 0.0 copy-start.2
  159.3 2.1 %copy.26 = bf16[56,2,8,384]{3,2,1,0:T(8,128)(2,1)} copy(bf16[56,2,8,384]{3,0,1,2:T(8,128)(2,1)} %bitcast.30) | data formatting | bytes 1376256 | tf_op jit(solution)/shard_map/transpose | solution.py:499
  161.5 0.0 copy-start.3
  161.5 0.0 copy-done.2
  161.5 0.1 copy.24
  161.6 0.9 reshape.27
  162.5 0.0 copy-done.3
  162.5 0.6 copy.28
  (2 shorter events, 0.0 us)
Async XLA Ops:
  0.6 1.0 copy-start
  0.6 4.2 %copy-start.1 = (bf16[1,56,1,16,672]{4,3,2,1,0:T(8,128)(2,1)S(1)}, bf16[1,56,1,16,672]{4,3,2,1,0:T(8,128)(2,1)}, u32[]{:S(2)}) copy-start(bf16[1,56,1,16,672]{4,3,2,1,0:T(8,128)(2,1)} %param.8) | copy-start | bytes 3612676
  159.3 2.2 %copy-start.2 = (f32[8,8,3,4,128]{4,3,2,1,0:T(4,128)S(1)}, f32[8,8,3,4,128]{4,3,2,1,0:T(4,128)}, u32[]{:S(2)}) copy-start(f32[8,8,3,4,128]{4,3,2,1,0:T(4,128)} %get-tuple-element.8) | copy-start | bytes 1179652
  161.5 1.0 copy-start.3

commit v3 on v2

--- a/solution.py
+++ b/solution.py
@@ -10,10 +10,10 @@
 
 
 def layer_kernel(
-    rows_ref, weight_ref, grad_ref, info_ref, gate_ref, tok_ref,
-    comb_ref, slot_grad_ref, router_ref,
-    weight, grads, tok_cols, made, arrived, passed_in, passed_out, mix, chosen, dots, total,
-    info, gg_out, gg_all, comb_out, comb_in, grad_out, part, from_dp, from_ctx,
+    rows_ref, weight_ref, grad_ref, ids_ref, router_ref, tok_ref,
+    comb_ref, slot_grad_ref, out_ref,
+    weight, grads, token_all, made, arrived, passed_in, passed_out, mix, chosen, dots, total,
+    row_gate, info, info_out, gates, gg_out, gg_all, comb_out, comb_in, grad_out, part, from_dp, from_ctx,
     load_sem, tok_sem, weight_sem, x_send, x_recv, z_send, z_recv, mg_send, mg_recv,
     pair_send, pair_recv, rg_send, rg_recv, gg_send, gg_recv,
     send1, recv1, send2, recv2, send3, recv3, send4, recv4,
@@ -59,11 +59,8 @@
         block = jnp.where(later < 0, last - n, inner)
         return block + flip * (last - 2 * block)
 
-    width = tok_cols.shape[1]
-    tok_load = pltpu.make_async_copy(
-        tok_ref.at[:, pl.ds(pl.multiple_of(z * width, 128), width)], tok_cols, tok_sem
-    )
-    tok_load.start()
+    width = token_all.shape[1] // n_z
+    tok_load = pltpu.make_async_copy(tok_ref, token_all, tok_sem)
 
     def weight_load(b):
         return pltpu.make_async_copy(
@@ -75,39 +72,27 @@
             grad_ref.at[:, pl.ds(pl.multiple_of(b * cols, 128), cols)], grads.at[b, own_rows], load_sem.at[b]
         )
 
+    barrier = pltpu.get_barrier_semaphore()
+    for count, where in ((n_z, at_z), (n_dp, at_dp), (n_ctx, at_ctx)):
+        @pl.loop(1, count)
+        def _(k):
+            pl.semaphore_signal(barrier, inc=1, device_id=where(k), device_id_type=MESH)
+
+    @pl.loop(1, n_z)
+    def _(k):
+        there = (dp, (1 - half) * n_q + q, lax.rem(z + k, n_z))
+        pl.semaphore_signal(barrier, inc=1, device_id=there, device_id_type=MESH)
+
     @pl.loop(0, n_z)
     def _(n):
         weight_load(block_at(n)).start()
 
+    tok_load.start()
+
     @pl.loop(0, n_z)
     def _(b):
         grad_load(b).start()
 
-    barrier = pltpu.get_barrier_semaphore()
-    for count, where in ((n_z, at_z), (n_dp, at_dp), (n_ctx, at_ctx)):
-        @pl.loop(1, count)
-        def _(k):
-            pl.semaphore_signal(barrier, inc=1, device_id=where(k), device_id_type=MESH)
-
-    @pl.loop(1, n_z)
-    def _(k):
-        there = (dp, (1 - half) * n_q + q, lax.rem(z + k, n_z))
-        pl.semaphore_signal(barrier, inc=1, device_id=there, device_id_type=MESH)
-
-    @pl.loop(0, n_z)
-    def _(b):
-        grad_load(b).wait()
-
-    pl.semaphore_wait(barrier, 2 * n_z + n_dp + n_ctx - 4)
-
-    info[half] = info_ref[half]
-    pair_info = remote(info_ref.at[1 - half], info.at[half], pair_send.at[0], pair_recv.at[0], pair)
-    pair_grad = remote(grads.at[z, own_rows], grads.at[z, own_rows], pair_send.at[1], pair_recv.at[1], pair)
-    got_info = remote(info_ref.at[half], info.at[1 - half], pair_send.at[0], pair_recv.at[0], pair)
-    got_grad = remote(grads.at[z, other_rows], grads.at[z, other_rows], pair_send.at[1], pair_recv.at[1], pair)
-    pair_info.start()
-    pair_grad.start()
-
     def x_copy(b, k):
         to = lax.rem(q + k, n_q)
         return remote(made.at[b, to], arrived.at[b, q], x_send.at[b, to], x_recv.at[b, q], at_q(k))
@@ -116,7 +101,7 @@
         come = lax.rem(q + k, n_q)
         return remote(made.at[b, come], arrived.at[b, come], x_send.at[b, come], x_recv.at[b, come], at_q(k))
 
-    def produce(n):
+    def multiply(n):
         b = block_at(n)
         weight_load(b).wait()
 
@@ -129,16 +114,58 @@
             )
             made[b, pl.ds(2 * r, 2)] = product.astype(jnp.bfloat16).reshape(2, size, cols)
 
+    def send(n):
+        b = block_at(n)
+
         @pl.loop(1, n_q)
         def _(k):
             x_copy(b, k).start()
 
         arrived[b, q] = made[b, q]
 
-    for n in range(AHEAD):
-        produce(n)
+    multiply(0)
+    pl.semaphore_wait(barrier, 2 * n_z + n_dp + n_ctx - 4)
+    send(0)
+
+    tok_load.wait()
+    logits = lax.dot_general(
+        router_ref[...], token_all[...], (((1,), (1,)), ((), ())), preferred_element_type=jnp.float32
+    )
+    experts = logits.shape[0]
+    names = lax.broadcasted_iota(jnp.int32, logits.shape, 0)
+    hits = jnp.zeros(logits.shape, jnp.float32)
+    for k in range(ids_ref.shape[0]):
+        hits = jnp.where(jnp.broadcast_to(ids_ref[k : k + 1, :], names.shape) == names, 1.0, hits)
+    hit = hits > 0.5
+    weights = jnp.where(hit, jnp.exp(logits), 0.0)
+    gate_values = weights / jnp.sum(weights, axis=0, keepdims=True)
+    gates[...] = gate_values
+    before = lax.broadcasted_iota(jnp.int32, (toks, toks), 0) < lax.broadcasted_iota(jnp.int32, (toks, toks), 1)
+    slot = jnp.dot(
+        hits.astype(jnp.bfloat16), jnp.where(before, 1.0, 0.0).astype(jnp.bfloat16), preferred_element_type=jnp.float32
+    )
+    capacity = rows_ref.shape[1] // 2
+    code = jnp.where(hit, slot + (half * capacity).astype(jnp.float32), -1.0)
+    for h in range(2):
+        info_out[h, 0] = gate_values[h * n_q : (h + 1) * n_q]
+        info_out[h, 1] = code[h * n_q : (h + 1) * n_q]
+    info[half] = info_out[half]
+    pair_info = remote(info_out.at[1 - half], info.at[half], pair_send.at[0], pair_recv.at[0], pair)
+    pair_grad = remote(grads.at[z, own_rows], grads.at[z, own_rows], pair_send.at[1], pair_recv.at[1], pair)
+    got_info = remote(info_out.at[half], info.at[1 - half], pair_send.at[0], pair_recv.at[0], pair)
+    got_grad = remote(grads.at[z, other_rows], grads.at[z, other_rows], pair_send.at[1], pair_recv.at[1], pair)
+    pair_info.start()
+
+    for n in range(1, AHEAD):
+        multiply(n)
+        send(n)
+
+    @pl.loop(0, n_z)
+    def _(b):
+        grad_load(b).wait()
 
     got_info.wait_recv()
+    pair_grad.start()
     per_q = rows_ref.shape[1]
     experts_here = n_q
 
@@ -156,13 +183,8 @@
     high = turned.astype(jnp.bfloat16)
     mix[0] = high
     mix[1] = (turned - high.astype(jnp.float32)).astype(jnp.bfloat16)
-    row_gate = jnp.sum(spread, axis=1, keepdims=True)
+    row_gate[...] = jnp.broadcast_to(jnp.sum(spread, axis=1, keepdims=True), row_gate.shape)
     dots[...] = jnp.zeros(dots.shape, jnp.float32)
-
-    got_grad.wait_recv()
-    picked_grad = jnp.dot(chosen[...], grads[z], preferred_element_type=jnp.float32) * row_gate
-    grad_out[...] = picked_grad.astype(jnp.bfloat16).reshape(grad_out.shape)
-    slot_grad_ref[q] = grad_out[q]
 
     def rg_copy(k):
         to = lax.rem(q + k, n_q)
@@ -171,10 +193,6 @@
     def rg_wait(k):
         come = lax.rem(q + k, n_q)
         return remote(grad_out.at[come], slot_grad_ref.at[come], rg_send.at[come], rg_recv.at[come], at_q(k))
-
-    @pl.loop(1, n_q)
-    def _(k):
-        rg_copy(k).start()
 
     def mg_copy(b, device):
         here = grads.at[b, other_rows]
@@ -226,8 +244,20 @@
             rows, grads[b], (((1,), (1,)), ((), ())), preferred_element_type=jnp.float32
         )
 
-    def z_copy(b, slot, device):
-        return remote(passed_out.at[b], passed_in.at[slot], z_send.at[b], z_recv.at[slot], device)
+    def far_dots(n):
+        @pl.when(z + n <= last)
+        def _():
+            add_dots(z + n)
+
+        @pl.when(z - n >= 0)
+        def _():
+            add_dots(z - n)
+
+    def z_copy(b, slot, s, device):
+        span = pl.ds(s * toks, toks)
+        return remote(
+            passed_out.at[b, span], passed_in.at[slot, span], z_send.at[b, s], z_recv.at[slot, s], device
+        )
 
     def x_wait_all(b):
         @pl.loop(1, n_q)
@@ -239,47 +269,65 @@
         b = block_at(n)
         x_wait_all(b)
 
-        @pl.when(n + AHEAD < n_z)
-        def _():
-            produce(n + AHEAD)
-
-        @pl.when(n < n_z // 2)
-        def _():
-            mg_step(2 * n)
-            mg_step(2 * n + 1)
-
         total[...] = mixed(b)
         up = b > z
-
-        @pl.when((up & (z > 0)) | (jnp.logical_not(up) & (z < last)))
-        def _():
-            z_copy(b, b, lower).wait_recv()
-            total[...] += passed_in[b].astype(jnp.float32)
-
-        passed_out[b] = total[...].astype(jnp.bfloat16)
-
-        @pl.when(up)
-        def _():
-            z_copy(b, b, upper).start()
-
-        @pl.when(b < z - 1)
-        def _():
-            z_copy(b, b, lower).start()
-
-        @pl.when(b == z - 1)
-        def _():
-            z_copy(b, n_z, lower).start()
+        fed = (up & (z > 0)) | (jnp.logical_not(up) & (z < last))
+        for s in range(2):
+            span = pl.ds(s * toks, toks)
+
+            @pl.when(fed)
+            def _():
+                z_copy(b, b, s, lower).wait_recv()
+                total[span, :] += passed_in[b, span].astype(jnp.float32)
+
+            passed_out[b, span] = total[span, :].astype(jnp.bfloat16)
+
+            @pl.when(up)
+            def _():
+                z_copy(b, b, s, upper).start()
+
+            @pl.when(b < z - 1)
+            def _():
+                z_copy(b, b, s, lower).start()
+
+            @pl.when(b == z - 1)
+            def _():
+                z_copy(b, n_z, s, lower).start()
+
+        @pl.when(n + AHEAD < n_z)
+        def _():
+            multiply(n + AHEAD)
+            send(n + AHEAD)
+
+        @pl.when(n == 0)
+        def _():
+            got_grad.wait_recv()
+            picked_grad = jnp.dot(chosen[...], grads[z], preferred_element_type=jnp.float32)
+            grad_out[...] = (picked_grad * row_gate[:, :1]).astype(jnp.bfloat16).reshape(grad_out.shape)
+            slot_grad_ref[q] = grad_out[q]
+
+        mg_step(n)
 
         @pl.when(n == n_z // 2)
         def _():
             @pl.loop(0, n_z // 2)
             def _(m):
-                add_dots(block_at(m))
+                early = block_at(m)
+
+                @pl.when((early - z <= n_z // 2) & (z - early <= n_z // 2))
+                def _():
+                    add_dots(early)
 
         @pl.when(n >= n_z // 2)
         def _():
             add_dots(b)
 
+        @pl.when(n > n_z // 2)
+        def _():
+            far_dots(n)
+
+    mg_step(last)
+    far_dots(last)
     x_wait_all(z)
     add_dots(z)
     gate_grad = jnp.where(chosen_mask(), dots[...].reshape(experts_here, per_q, 2 * toks), 0.0)
@@ -301,22 +349,27 @@
     def _(k):
         gg_copy(k, spot).start()
 
+    @pl.loop(1, n_q)
+    def _(k):
+        rg_copy(k).start()
+
     total[...] = mixed(z)
 
-    @pl.when(z > 0)
-    def _():
-        z_copy(z, z, lower).wait_recv()
-        total[...] += passed_in[z].astype(jnp.float32)
-
-    @pl.when(z < last)
-    def _():
-        z_copy(z, n_z, upper).wait_recv()
-        total[...] += passed_in[n_z].astype(jnp.float32)
+    for s in range(2):
+        span = pl.ds(s * toks, toks)
+
+        @pl.when(z > 0)
+        def _():
+            z_copy(z, z, s, lower).wait_recv()
+            total[span, :] += passed_in[z, span].astype(jnp.float32)
+
+        @pl.when(z < last)
+        def _():
+            z_copy(z, n_z, s, upper).wait_recv()
+            total[span, :] += passed_in[n_z, span].astype(jnp.float32)
 
     comb_out[...] = total[other_rows, :].astype(jnp.bfloat16)
     pair_comb = remote(comb_out, comb_in, pair_send.at[2], pair_recv.at[2], pair)
-    pair_comb.start()
-
     @pl.loop(1, 2 * n_z)
     def _(k):
         gg_copy(k, lax.rem(spot + k, 2 * n_z)).wait_recv()
@@ -328,20 +381,18 @@
             summed = summed + gg_all[h * n_z + k]
         parts.append(summed)
     gate_grad = jnp.concatenate(parts, axis=0)
-    gates = gate_ref[...]
-    mix_term = jnp.sum(gates * gate_grad, axis=0, keepdims=True)
-    logit_grad = gates * (gate_grad - mix_term)
+    gate_values = gates[...]
+    mix_term = jnp.sum(gate_values * gate_grad, axis=0, keepdims=True)
+    logit_grad = gate_values * (gate_grad - mix_term)
     high = logit_grad.astype(jnp.bfloat16)
     rest = logit_grad - high.astype(jnp.float32)
     middle = rest.astype(jnp.bfloat16)
     low = (rest - middle.astype(jnp.float32)).astype(jnp.bfloat16)
-    tok_load.wait()
-    token_cols = tok_cols[...]
+    token_cols = token_all[:, pl.ds(pl.multiple_of(z * width, 128), width)]
     product = jnp.dot(low, token_cols, preferred_element_type=jnp.float32)
     product += jnp.dot(middle, token_cols, preferred_element_type=jnp.float32)
     product += jnp.dot(high, token_cols, preferred_element_type=jnp.float32)
     product = product * (1.0 / toks)
-    experts = product.shape[0]
     each, lanes = experts // n_dp, width // 128
     for e in range(experts):
         for k in range(lanes):
@@ -375,9 +426,10 @@
     summed = from_ctx[0]
     for k in range(1, n_ctx):
         summed = summed + from_ctx[k]
-    router_ref[dp, z] = summed
-    exchange(n_z, z, at_z, lambda k: router_ref.at[dp, z], lambda k: router_ref.at[dp, k], send3, recv3)
-    exchange(n_dp, dp, at_dp, lambda k: router_ref.at[dp], lambda k: router_ref.at[k], send4, recv4)
+    out_ref[dp, z] = summed
+    exchange(n_z, z, at_z, lambda k: out_ref.at[dp, z], lambda k: out_ref.at[dp, k], send3, recv3)
+    pair_comb.start()
+    exchange(n_dp, dp, at_dp, lambda k: out_ref.at[dp], lambda k: out_ref.at[k], send4, recv4)
 
     remote(comb_out, comb_in, pair_send.at[2], pair_recv.at[2], pair).wait_recv()
     comb_ref[...] = (total[own_rows, :] + comb_in[...].astype(jnp.float32)).astype(jnp.bfloat16)
@@ -408,16 +460,17 @@
 
         @pl.when(j != z)
         def _():
-            z_copy(j, j, lower).wait_send()
-
-
-def layer(rows, weight, grad, info, gates, tokens):
+            z_copy(j, j, 0, lower).wait_send()
+            z_copy(j, j, 1, lower).wait_send()
+
+
+def layer(rows, weight, grad, ids, router_weight, tokens):
     n_dp, n_ctx, n_z = lax.axis_size("dp"), lax.axis_size("ctx"), lax.axis_size("tp")
     n_q = n_ctx // 2
     per_q, depth = rows.shape[1:]
     full = weight.shape[1]
     cols = full // n_z
-    experts, toks = gates.shape
+    experts, toks = router_weight.shape[0], tokens.shape[0]
     width = tokens.shape[1] // n_z
     each, lanes = experts // n_dp, width // 128
     chunk = (each * lanes // 4, 4, 128)
@@ -428,7 +481,7 @@
     scratch = [
         pltpu.VMEM((n_z, depth, cols), bf16),
         pltpu.VMEM((n_z, 2 * toks, cols), bf16),
-        pltpu.VMEM((toks, width), bf16),
+        pltpu.VMEM(tokens.shape, bf16),
         pltpu.VMEM((n_z, n_q, per_q, cols), bf16),
         pltpu.VMEM((n_z, n_q, per_q, cols), bf16),
         pltpu.VMEM((n_z + 1, 2 * toks, cols), bf16),
@@ -437,7 +490,10 @@
         pltpu.VMEM((n_q * per_q, 2 * toks), bf16),
         pltpu.VMEM((n_q * per_q, 2 * toks), f32),
         pltpu.VMEM((2 * toks, cols), f32),
+        pltpu.VMEM((n_q * per_q, 128), f32),
         pltpu.VMEM((2, 2, n_q, toks), f32),
+        pltpu.VMEM((2, 2, n_q, toks), f32),
+        pltpu.VMEM((experts, toks), f32),
         pltpu.VMEM((2, n_q, toks), f32),
         pltpu.VMEM((2 * n_z, n_q, toks), f32),
         pltpu.VMEM((toks, cols), bf16),
@@ -448,7 +504,7 @@
         pltpu.VMEM((n_ctx,) + chunk, f32),
         dma((n_z,)), dma, dma((n_z,)),
         dma((n_z, n_q)), dma((n_z, n_q)),
-        dma((n_z,)), dma((n_z + 1,)),
+        dma((n_z, 2)), dma((n_z + 1, 2)),
         dma((2 * n_z,)), dma((n_z,)),
         dma((3,)), dma((3,)),
         dma((n_q,)), dma((n_q,)),
@@ -468,34 +524,21 @@
         scratch_shapes=scratch,
         compiler_params=pltpu.CompilerParams(collective_id=1, has_side_effects=True, vmem_limit_bytes=56 << 20),
         name="layer",
-    )(rows, weight, grad, info, gates, tokens)
+    )(rows, weight, grad, ids, router_weight, tokens)
 
 
 def per_device(tokens, router_weight, expert_hidden, down_weight, expert_ids, mixed_grad):
-    ctx_ranks, tp_ranks, dp_ranks = lax.axis_size("ctx"), lax.axis_size("tp"), lax.axis_size("dp")
-    half = lax.axis_index("ctx") // (ctx_ranks // 2)
+    tp_ranks, dp_ranks = lax.axis_size("tp"), lax.axis_size("dp")
     hidden = expert_hidden[0, :, 0]
     capacity, sources, depth = hidden.shape
     experts = router_weight.shape[1]
-    tok_count = tokens.shape[0]
     group = sources // 2
     rows = hidden.reshape(capacity, 2, group, depth).transpose(2, 1, 0, 3)
     rows = rows.reshape(group, 2 * capacity, depth)
 
-    logits = lax.dot_general(
-        router_weight, tokens, (((0,), (1,)), ((), ())), preferred_element_type=jnp.float32
+    combined, slot_grads, router = layer(
+        rows, down_weight[0], mixed_grad, expert_ids.T, router_weight.T, tokens
     )
-    names = jnp.arange(experts, dtype=jnp.int32)[:, None]
-    hit = jnp.any(expert_ids.T[:, None, :] == names[None], axis=0)
-    weights = jnp.where(hit, jnp.exp(logits), 0.0)
-    gates = weights / jnp.sum(weights, axis=0, keepdims=True)
-    place = jnp.arange(tok_count, dtype=jnp.int32)
-    earlier = (place[:, None] < place[None, :]).astype(jnp.bfloat16)
-    slot = jnp.dot(hit.astype(jnp.bfloat16), earlier, preferred_element_type=jnp.float32)
-    code = jnp.where(hit, slot + (half * capacity).astype(jnp.float32), -1.0)
-    info = jnp.stack([gates.reshape(2, group, tok_count), code.reshape(2, group, tok_count)], axis=1)
-
-    combined, slot_grads, router = layer(rows, down_weight[0], mixed_grad, info, gates, tokens)
     slot_grads = slot_grads.reshape(group, 2, capacity, slot_grads.shape[-1]).transpose(2, 1, 0, 3)
     row_grads = slot_grads.reshape(1, capacity, 1, sources, slot_grads.shape[-1])
     each = experts // dp_ranks

time: 165 us -> 148 us (0.90)
  Pallas kernels: 153 us -> 140 us
  matrix products: 2.08 us -> 0 us
  other arithmetic: 2.04 us -> 0 us
    pallas_call x1, Pallas kernels: 153 us -> 140 us  [layer(): pl.pallas_call(layer_kernel, out_shape=(jax.ShapeDtypeStruct((toks, cols)...]
    dot_general x2 -> x0, matrix products: 2.08 us -> none  [the longest x1 1.94 us: per_device(): lax.dot_general(router_weight, tokens, (((0,), (1,)), ((), ())), preferre...]
where the time goes in v3:
time: 148 us; the launch traced here: 147 us
  Pallas kernels  140 us (95%)
  local copies, waits for them, and re-layouts  6.61 us (4%)
    pallas_call x1, Pallas kernels, layer(): pl.pallas_call(layer_kernel, out_shape=(jax.ShapeDtypeStruct((toks, cols)...  140 us

profile of v3, /device:TPU:6, one launch (start us, length us, event | category | flops | bytes accessed | tf_op | source)
XLA Modules:
  0.0 147.1 jit_solution(3258096754117925135)
XLA Ops:
  0.6 2.8 %copy.12 = bf16[56,2,8,672]{3,0,1,2:T(8,128)(2,1)} copy(bf16[56,2,8,672]{3,2,1,0:T(8,128)(2,1)} %bitcast.20) | data formatting | bytes 2408448 | tf_op jit(solution)/shard_map/reshape;squeeze | solution.py:536
  3.5 139.8 %layer.1 = (bf16[128,384]{1,0:T(8,128)(2,1)}, bf16[8,112,384]{2,1,0:T(8,128)(2,1)}, f32[8,8,3,4,128]{4,3,2,1,0:T(4,128)}) custom-call(bf16[8,112,672]{2,1,0:T(8,128)(2,1)} %bitcast.17, bf16[672,3072]{1,0:T(8,128)(2,1)} %bitcast.18, bf16[128,3072]{1,0:T(8,128)(2,1)} %grad_ref.1, s32[4,128]{1,0:T(4,128)} %bitcast.25, bf16[16,6144]{1,0:T(8,128)(2,1)} %bitcast.24, ...), custom_call_target="tpu_custom_call" | custom-call | tf_op jit(solution)/shard_map/layer/pallas_call | solution.py:515
  143.3 0.0 copy-start
  143.3 2.1 %copy.17 = bf16[56,2,8,384]{3,2,1,0:T(8,128)(2,1)} copy(bf16[56,2,8,384]{3,0,1,2:T(8,128)(2,1)} %bitcast.22) | data formatting | bytes 1376256 | tf_op jit(solution)/shard_map/transpose | solution.py:542
  145.5 0.0 copy-start.1
  145.5 0.0 copy-done
  145.5 0.1 copy.15
  145.6 0.9 reshape.25
  146.4 0.0 copy-done.1
  146.5 0.6 copy.19
  (1 shorter events, 0.0 us)
Async XLA Ops:
  143.3 2.2 %copy-start = (f32[8,8,3,4,128]{4,3,2,1,0:T(4,128)S(1)}, f32[8,8,3,4,128]{4,3,2,1,0:T(4,128)}, u32[]{:S(2)}) copy-start(f32[8,8,3,4,128]{4,3,2,1,0:T(4,128)} %get-tuple-element.8) | copy-start | bytes 1179652
  145.5 1.0 copy-start.1

commit v4 on v3

--- a/solution.py
+++ b/solution.py
@@ -264,11 +264,8 @@
         def _(k):
             x_wait(b, k).wait_recv()
 
-    @pl.loop(0, last)
-    def _(n):
+    def pass_on(n):
         b = block_at(n)
-        x_wait_all(b)
-
         total[...] = mixed(b)
         up = b > z
         fed = (up & (z > 0)) | (jnp.logical_not(up) & (z < last))
@@ -294,6 +291,32 @@
             def _():
                 z_copy(b, n_z, s, lower).start()
 
+    def gather_dots(n, b):
+        mg_step(n)
+
+        @pl.when(n == n_z // 2)
+        def _():
+            @pl.loop(0, n_z // 2)
+            def _(m):
+                early = block_at(m)
+
+                @pl.when((early - z <= n_z // 2) & (z - early <= n_z // 2))
+                def _():
+                    add_dots(early)
+
+        @pl.when(n >= n_z // 2)
+        def _():
+            add_dots(b)
+
+        @pl.when(n > n_z // 2)
+        def _():
+            far_dots(n)
+
+    @pl.loop(0, last)
+    def _(n):
+        b = block_at(n)
+        x_wait_all(b)
+
         @pl.when(n + AHEAD < n_z)
         def _():
             multiply(n + AHEAD)
@@ -306,25 +329,11 @@
             grad_out[...] = (picked_grad * row_gate[:, :1]).astype(jnp.bfloat16).reshape(grad_out.shape)
             slot_grad_ref[q] = grad_out[q]
 
-        mg_step(n)
-
-        @pl.when(n == n_z // 2)
-        def _():
-            @pl.loop(0, n_z // 2)
-            def _(m):
-                early = block_at(m)
-
-                @pl.when((early - z <= n_z // 2) & (z - early <= n_z // 2))
-                def _():
-                    add_dots(early)
-
-        @pl.when(n >= n_z // 2)
-        def _():
-            add_dots(b)
-
-        @pl.when(n > n_z // 2)
-        def _():
-            far_dots(n)
+        gather_dots(n, b)
+
+        @pl.when(n > 0)
+        def _():
+            pass_on(n - 1)
 
     mg_step(last)
     far_dots(last)
@@ -353,23 +362,8 @@
     def _(k):
         rg_copy(k).start()
 
-    total[...] = mixed(z)
-
-    for s in range(2):
-        span = pl.ds(s * toks, toks)
-
-        @pl.when(z > 0)
-        def _():
-            z_copy(z, z, s, lower).wait_recv()
-            total[span, :] += passed_in[z, span].astype(jnp.float32)
-
-        @pl.when(z < last)
-        def _():
-            z_copy(z, n_z, s, upper).wait_recv()
-            total[span, :] += passed_in[n_z, span].astype(jnp.float32)
-
-    comb_out[...] = total[other_rows, :].astype(jnp.bfloat16)
-    pair_comb = remote(comb_out, comb_in, pair_send.at[2], pair_recv.at[2], pair)
+    pass_on(last - 1)
+
     @pl.loop(1, 2 * n_z)
     def _(k):
         gg_copy(k, lax.rem(spot + k, 2 * n_z)).wait_recv()
@@ -399,7 +393,28 @@
             row = (e % each) * lanes + k
             part[e // each, row // 4, row % 4 : row % 4 + 1, :] = product[e : e + 1, k * 128 : (k + 1) * 128]
 
-    def exchange(count, me, where, source, target, send, recv):
+    pair_comb = remote(comb_out, comb_in, pair_send.at[2], pair_recv.at[2], pair)
+
+    def finish_own():
+        total[...] = mixed(z)
+
+        for s in range(2):
+            span = pl.ds(s * toks, toks)
+
+            @pl.when(z > 0)
+            def _():
+                z_copy(z, z, s, lower).wait_recv()
+                total[span, :] += passed_in[z, span].astype(jnp.float32)
+
+            @pl.when(z < last)
+            def _():
+                z_copy(z, n_z, s, upper).wait_recv()
+                total[span, :] += passed_in[n_z, span].astype(jnp.float32)
+
+        comb_out[...] = total[other_rows, :].astype(jnp.bfloat16)
+        pair_comb.start()
+
+    def exchange(count, me, where, source, target, send, recv, meanwhile=None):
         def copy(k, slot):
             to = lax.rem(me + k, count)
             return remote(source(to), target(slot), send.at[to], recv.at[slot], where(k))
@@ -407,6 +422,9 @@
         @pl.loop(1, count)
         def _(k):
             copy(k, me).start()
+
+        if meanwhile is not None:
+            meanwhile()
 
         @pl.loop(1, count)
         def _(k):
@@ -422,13 +440,12 @@
     for k in range(1, n_dp):
         summed = summed + from_dp[k]
     from_ctx[ctx] = summed
-    exchange(n_ctx, ctx, at_ctx, lambda k: from_ctx.at[ctx], lambda k: from_ctx.at[k], send2, recv2)
+    exchange(n_ctx, ctx, at_ctx, lambda k: from_ctx.at[ctx], lambda k: from_ctx.at[k], send2, recv2, finish_own)
     summed = from_ctx[0]
     for k in range(1, n_ctx):
         summed = summed + from_ctx[k]
     out_ref[dp, z] = summed
     exchange(n_z, z, at_z, lambda k: out_ref.at[dp, z], lambda k: out_ref.at[dp, k], send3, recv3)
-    pair_comb.start()
     exchange(n_dp, dp, at_dp, lambda k: out_ref.at[dp], lambda k: out_ref.at[k], send4, recv4)
 
     remote(comb_out, comb_in, pair_send.at[2], pair_recv.at[2], pair).wait_recv()

time: 148 us -> 150 us (1.014)
  Pallas kernels: 140 us -> 142 us
    pallas_call x1, Pallas kernels: 140 us -> 142 us  [layer(): pl.pallas_call(layer_kernel, out_shape=(jax.ShapeDtypeStruct((toks, cols)...]
where the time goes in v4:
time: 150 us; the launch traced here: 149 us
  Pallas kernels  142 us (95%)
  local copies, waits for them, and re-layouts  6.61 us (4%)
    pallas_call x1, Pallas kernels, layer(): pl.pallas_call(layer_kernel, out_shape=(jax.ShapeDtypeStruct((toks, cols)...  142 us

profile of v4, /device:TPU:6, one launch (start us, length us, event | category | flops | bytes accessed | tf_op | source)
XLA Modules:
  0.0 149.4 jit_solution(2374958917085235814)
XLA Ops:
  0.6 2.8 %copy.12 = bf16[56,2,8,672]{3,0,1,2:T(8,128)(2,1)} copy(bf16[56,2,8,672]{3,2,1,0:T(8,128)(2,1)} %bitcast.20) | data formatting | bytes 2408448 | tf_op jit(solution)/shard_map/reshape;squeeze | solution.py:553
  3.5 142.1 %layer.1 = (bf16[128,384]{1,0:T(8,128)(2,1)}, bf16[8,112,384]{2,1,0:T(8,128)(2,1)}, f32[8,8,3,4,128]{4,3,2,1,0:T(4,128)}) custom-call(bf16[8,112,672]{2,1,0:T(8,128)(2,1)} %bitcast.17, bf16[672,3072]{1,0:T(8,128)(2,1)} %bitcast.18, bf16[128,3072]{1,0:T(8,128)(2,1)} %grad_ref.1, s32[4,128]{1,0:T(4,128)} %bitcast.25, bf16[16,6144]{1,0:T(8,128)(2,1)} %bitcast.24, ...), custom_call_target="tpu_custom_call" | custom-call | tf_op jit(solution)/shard_map/layer/pallas_call | solution.py:532
  145.6 0.0 copy-start
  145.6 2.1 %copy.17 = bf16[56,2,8,384]{3,2,1,0:T(8,128)(2,1)} copy(bf16[56,2,8,384]{3,0,1,2:T(8,128)(2,1)} %bitcast.22) | data formatting | bytes 1376256 | tf_op jit(solution)/shard_map/transpose | solution.py:559
  147.7 0.0 copy-start.1
  147.7 0.0 copy-done
  147.8 0.1 copy.15
  147.9 0.9 reshape.25
  148.7 0.0 copy-done.1
  148.7 0.6 copy.19
  (1 shorter events, 0.0 us)
Async XLA Ops:
  145.6 2.2 %copy-start = (f32[8,8,3,4,128]{4,3,2,1,0:T(4,128)S(1)}, f32[8,8,3,4,128]{4,3,2,1,0:T(4,128)}, u32[]{:S(2)}) copy-start(f32[8,8,3,4,128]{4,3,2,1,0:T(4,128)} %get-tuple-element.8) | copy-start | bytes 1179652
  147.7 1.0 copy-start.1

commit v5 on v3

--- a/solution.py
+++ b/solution.py
@@ -13,7 +13,7 @@
     rows_ref, weight_ref, grad_ref, ids_ref, router_ref, tok_ref,
     comb_ref, slot_grad_ref, out_ref,
     weight, grads, token_all, made, arrived, passed_in, passed_out, mix, chosen, dots, total,
-    row_gate, info, info_out, gates, gg_out, gg_all, comb_out, comb_in, grad_out, part, from_dp, from_ctx,
+    row_gate, info, info_out, gates, gg_out, gg_all, comb_out, comb_in, grad_out, part, from_dp, from_ctx, packed,
     load_sem, tok_sem, weight_sem, x_send, x_recv, z_send, z_recv, mg_send, mg_recv,
     pair_send, pair_recv, rg_send, rg_recv, gg_send, gg_recv,
     send1, recv1, send2, recv2, send3, recv3, send4, recv4,
@@ -399,7 +399,7 @@
             row = (e % each) * lanes + k
             part[e // each, row // 4, row % 4 : row % 4 + 1, :] = product[e : e + 1, k * 128 : (k + 1) * 128]
 
-    def exchange(count, me, where, source, target, send, recv):
+    def exchange(count, me, where, source, target, send, recv, meanwhile=None):
         def copy(k, slot):
             to = lax.rem(me + k, count)
             return remote(source(to), target(slot), send.at[to], recv.at[slot], where(k))
@@ -407,6 +407,9 @@
         @pl.loop(1, count)
         def _(k):
             copy(k, me).start()
+
+        if meanwhile is not None:
+            meanwhile()
 
         @pl.loop(1, count)
         def _(k):
@@ -426,9 +429,11 @@
     summed = from_ctx[0]
     for k in range(1, n_ctx):
         summed = summed + from_ctx[k]
-    out_ref[dp, z] = summed
-    exchange(n_z, z, at_z, lambda k: out_ref.at[dp, z], lambda k: out_ref.at[dp, k], send3, recv3)
-    pair_comb.start()
+    packed[...] = jnp.zeros(packed.shape, jnp.float32)
+    for k in range(summed.shape[0]):
+        packed[4 * k : 4 * k + 4, :] = summed[k]
+    out_ref[dp, z] = packed[...].astype(jnp.bfloat16)
+    exchange(n_z, z, at_z, lambda k: out_ref.at[dp, z], lambda k: out_ref.at[dp, k], send3, recv3, pair_comb.start)
     exchange(n_dp, dp, at_dp, lambda k: out_ref.at[dp], lambda k: out_ref.at[k], send4, recv4)
 
     remote(comb_out, comb_in, pair_send.at[2], pair_recv.at[2], pair).wait_recv()
@@ -474,6 +479,7 @@
     width = tokens.shape[1] // n_z
     each, lanes = experts // n_dp, width // 128
     chunk = (each * lanes // 4, 4, 128)
+    padded = -(-each * lanes // 16) * 16
     vmem = pl.BlockSpec(memory_space=pltpu.VMEM)
     anywhere = pl.BlockSpec(memory_space=pl.ANY)
     bf16, f32 = jnp.bfloat16, jnp.float32
@@ -502,6 +508,7 @@
         pltpu.VMEM((n_dp,) + chunk, f32),
         pltpu.VMEM((n_dp,) + chunk, f32),
         pltpu.VMEM((n_ctx,) + chunk, f32),
+        pltpu.VMEM((padded, 128), f32),
         dma((n_z,)), dma, dma((n_z,)),
         dma((n_z, n_q)), dma((n_z, n_q)),
         dma((n_z, 2)), dma((n_z + 1, 2)),
@@ -517,7 +524,7 @@
         out_shape=(
             jax.ShapeDtypeStruct((toks, cols), bf16),
             jax.ShapeDtypeStruct((n_q, per_q, cols), bf16),
-            jax.ShapeDtypeStruct((n_dp, n_z) + chunk, f32),
+            jax.ShapeDtypeStruct((n_dp, n_z, padded, 128), bf16),
         ),
         in_specs=[vmem, anywhere, anywhere, vmem, vmem, anywhere],
         out_specs=(vmem, vmem, vmem),
@@ -542,7 +549,9 @@
     slot_grads = slot_grads.reshape(group, 2, capacity, slot_grads.shape[-1]).transpose(2, 1, 0, 3)
     row_grads = slot_grads.reshape(1, capacity, 1, sources, slot_grads.shape[-1])
     each = experts // dp_ranks
-    router = router.reshape(dp_ranks, tp_ranks, each, -1, 128).transpose(0, 2, 1, 3, 4)
+    lanes = tokens.shape[1] // tp_ranks // 128
+    router = router[:, :, : each * lanes].astype(jnp.float32)
+    router = router.reshape(dp_ranks, tp_ranks, each, lanes, 128).transpose(0, 2, 1, 3, 4)
     router_grad = router.reshape(experts, tokens.shape[1]).T
     return (combined, row_grads, router_grad)
 

time: 148 us -> 148 us (level)
  no operation moved by 1% of the time
where the time goes in v5:
time: 148 us; the launch traced here: 147 us
  Pallas kernels  139 us (94%)
  local copies, waits for them, and re-layouts  6.64 us (4%)
    pallas_call x1, Pallas kernels, layer(): pl.pallas_call(layer_kernel, out_shape=(jax.ShapeDtypeStruct((toks, cols)...  139 us

profile of v5, /device:TPU:6, one launch (start us, length us, event | category | flops | bytes accessed | tf_op | source)
XLA Modules:
  0.0 146.8 jit_solution(1699300996736280140)
XLA Ops:
  0.6 2.8 %copy.16 = bf16[56,2,8,672]{3,0,1,2:T(8,128)(2,1)} copy(bf16[56,2,8,672]{3,2,1,0:T(8,128)(2,1)} %bitcast.20) | data formatting | bytes 2408448 | tf_op jit(solution)/shard_map/reshape;squeeze | solution.py:543
  3.5 138.5 %layer.1 = (bf16[128,384]{1,0:T(8,128)(2,1)}, bf16[8,112,384]{2,1,0:T(8,128)(2,1)}, bf16[8,8,16,128]{3,2,1,0:T(8,128)(2,1)}) custom-call(bf16[8,112,672]{2,1,0:T(8,128)(2,1)} %bitcast.17, bf16[672,3072]{1,0:T(8,128)(2,1)} %bitcast.18, bf16[128,3072]{1,0:T(8,128)(2,1)} %grad_ref.1, s32[4,128]{1,0:T(4,128)} %bitcast.25, bf16[16,6144]{1,0:T(8,128)(2,1)} %bitcast.24, ...), custom_call_target="tpu_custom_call" | custom-call | tf_op jit(solution)/shard_map/layer/pallas_call | solution.py:522
  142.0 2.1 %copy.21 = bf16[56,2,8,384]{3,2,1,0:T(8,128)(2,1)} copy(bf16[56,2,8,384]{3,0,1,2:T(8,128)(2,1)} %bitcast.22) | data formatting | bytes 1376256 | tf_op jit(solution)/shard_map/transpose | solution.py:549
  144.1 1.0 slice_convert_fusion
  145.1 0.0 copy-start
  145.1 0.1 copy.18
  145.2 0.1 copy.19
  145.3 0.9 reshape.28
  146.2 0.0 copy-done
  146.2 0.6 copy.23
Async XLA Ops:
  145.1 1.1 copy-start
